TPU v7x, 512 devices: a whole 4x8x8 slice. The times are simulated.
512 devices in a mesh: row: 32 (over y, x), col: 16 (over z, core).
Axes of the slice: x: 4, y: 8, z: 8, core: 2. Of those that a mesh axis runs over, the one named last changes fastest.
Arguments:
- front: float32 [2, 8192, 8192], P(None, 'row', 'col'), may hold values from -6 to 6
- panel: float32 [2, 8192, 256], P(None, ('row', 'col')), may hold values from -1.5 to 1.5
- inverses: float32 [2, 2, 128, 128], replicated, may hold values from -2 to 2
- coupling: float32 [2, 128, 128], replicated, may hold values from -0.5 to 0.5
- channels: float32 [2, 8192, 512], P(None, ('row', 'col')), may hold values from -0.0625 to 0.0625
Outputs:
- schur: float32 [2, 8192, 8192], P(None, 'row', 'col')
- projected: float32 [2, 512, 512], replicated
All inputs are finite; a program needn't handle non-finite values.
Results may differ from a plain program's by a relative error of at most 0.00016.
Values sent between devices are 32-bit elements; how exact they have to be, the bound alone decides.
A program may use at most 64 MiB of HBM per device.

v0:
```python
import jax
import jax.numpy as jnp
from jax import lax
from jax.sharding import Mesh
from jax.sharding import PartitionSpec as P

COL = ("col_0", "col_1")
ROW = ("row_0", "row_1")
ROW_COL = ("row_0", "row_1", "col_0", "col_1")


HIGH = lax.Precision.HIGHEST


def sent_together(arrays, axis, dim, along):
    both = jnp.concatenate(arrays, axis=along)
    result, at, gathered = (lax.all_gather(both, axis, axis=dim, tiled=True), 0, [])
    for a in arrays:
        gathered.append(lax.slice_in_dim(result, at, at + a.shape[along], axis=along))
        at += a.shape[along]
    return tuple(gathered)


def broadcast_by_axis(x, axes, root):
    x = jnp.where(lax.axis_index(axes) == root, x, jnp.zeros_like(x))
    for axis in axes:
        x = lax.psum(x, axis)
    return x


def in_blocks(x, dim, peers):
    before, after = (x.shape[:dim], x.shape[dim + 1 :])
    return jnp.moveaxis(x.reshape(*before, peers, -1, *after), dim, 0)


def summed_on_arrival(x, axis, dim):
    blocks = in_blocks(x, dim, lax.axis_size(axis))
    arrived = lax.all_to_all(blocks, axis, split_axis=0, concat_axis=0, tiled=True)
    return arrived.sum(axis=0)


def summed_rows(x, axes, dim):
    far, near = axes
    own = summed_on_arrival(in_blocks(x, dim, lax.axis_size(far)), near, dim + 1)
    return jnp.sum(lax.all_to_all(own, far, 0, 0, tiled=True), axis=0)


def padded_to(lines, peers):
    spare = -len(lines) % peers
    return jnp.pad(lines, [(0, spare)] + [(0, 0)] * (lines.ndim - 1))


def copy_for_each(x, axis):
    peers = lax.axis_size(axis)
    return lax.all_to_all(jnp.broadcast_to(x[None], (peers, *x.shape)), axis, 0, 0, tiled=True)


def laid_out(blocks, dim):
    dims = list(blocks.shape[1:])
    dims[dim] *= blocks.shape[0]
    return jnp.moveaxis(blocks, 0, dim).reshape(dims)


def whole_of(x, axes, dim):
    far, near = axes
    blocks = copy_for_each(copy_for_each(x, far), near)
    return laid_out(blocks.swapaxes(0, 1).reshape(-1, *x.shape), dim)


def total_of(x, axes):
    lines = x.reshape(-1, x.shape[-1])
    own = summed_rows(padded_to(lines, lax.axis_size(axes[0]) * lax.axis_size(axes[1])), axes, 0)
    whole = whole_of(own, axes, 0)
    return whole[: len(lines)].reshape(x.shape)


def real_dot(left, right):
    return jnp.dot(left, right, precision=HIGH, preferred_element_type=jnp.float32)


def complex_dot(left, right):
    return jnp.stack(
        [
            real_dot(left[0], right[0]) - real_dot(left[1], right[1]),
            real_dot(left[0], right[1]) + real_dot(left[1], right[0]),
        ]
    )


def complex_dot_nt(left, right):
    return complex_dot(left, jnp.swapaxes(right, 1, 2))


def complex_dot_tn(left, right):
    return complex_dot(jnp.swapaxes(left, 1, 2), right)


def local(front, panel, inverses, coupling, channels):
    width = inverses.shape[-1]
    first = panel[:, :, :width]
    second = panel[:, :, width:] - complex_dot(first, complex_dot_nt(inverses[0], coupling))
    columns = jnp.concatenate([first, second], axis=2)
    scaled = jnp.concatenate(
        [complex_dot(first, inverses[0]), complex_dot(second, inverses[1])], axis=2
    )
    scaled_rows, column_rows, chan_rows = sent_together((scaled, columns, channels), COL, 1, 2)
    ratio = lax.axis_size(ROW) // lax.axis_size(COL)
    base = lax.axis_index(COL) * ratio
    panel_parts = []
    chan_parts = []
    for offset in range(ratio):
        got_panel, got_chan = (
            broadcast_by_axis(column_rows, ROW, base + offset),
            broadcast_by_axis(chan_rows, ROW, base + offset),
        )
        panel_parts.append(got_panel)
        chan_parts.append(got_chan)
    panel_cols = jnp.concatenate(panel_parts, axis=1)
    chan_cols = jnp.concatenate(chan_parts, axis=1)
    schur = front - complex_dot_nt(scaled_rows, panel_cols)
    applied = complex_dot(schur, chan_cols)
    partial_matrix = complex_dot_tn(chan_rows, applied)
    projected = total_of(partial_matrix, ("row_0", ("row_1", "col_0", "col_1")))
    return (schur, projected)


def solution(mesh):
    finer = Mesh(mesh.devices.reshape(8, 4, 8, 2), ("row_0", "row_1", "col_0", "col_1"))
    in_specs = (P(None, ROW, COL), P(None, ROW_COL, None), P(), P(), P(None, ROW_COL, None))
    out_specs = (P(None, ROW, COL), P())
    return jax.shard_map(local, mesh=finer, in_specs=in_specs, out_specs=out_specs, check_vma=False)
```

profile of v0, /device:TPU:1, one launch (start us, length us, event | category | flops | bytes accessed | tf_op | source)
XLA Modules:
  0.0 437.2 jit_solution(12309153181070667556)
XLA Ops:
  7.2 0.0 copy-start.6
  7.2 0.0 all-gather.2.cloned.1.call-start
  7.2 1.0 fusion.24
  8.2 1.0 fusion.32
  9.3 1.2 fusion.27
  10.4 1.1 fusion.29
  11.6 1.1 convolution_add_fusion.3
  12.7 0.9 fusion.50
  13.6 1.2 convolution_subtract_fusion.3
  14.7 0.9 fusion.52
  15.6 0.9 fusion.6
  16.4 0.9 fusion.7
  17.3 0.7 maximum_subtract_fusion.1
  18.1 1.0 fusion.16
  19.0 1.0 fusion.20
  20.1 1.0 fusion.8
  21.1 1.0 fusion.9
  22.1 1.0 fusion.4
  23.1 1.0 fusion.5
  24.2 0.7 constant_dynamic-update-slice_fusion.2
  24.9 0.0 copy-done.6
  24.9 0.0 copy-start.7
  24.9 0.6 copy-done.7
  25.6 0.0 all-gather.2.cloned.1.call-update
  25.6 0.0 all-reduce.5.cloned.1.call-start
  25.7 49.2 %all-gather.2.cloned.1.call-done = f32[2,256,1024]{2,1,0:T(8,128)} async-done(((f32[2,16,1024]{2,1,0:T(8,128)}), f32[2,256,1024]{2,1,0:T(8,128)}) %all-gather.2.cloned.1.call-update) | async-done | bytes 2097168 | tf_op jit(solution)/shard_map/all_gather | solution.py:17
  74.9 2.1 slice_select_fusion.3
  77.0 3.0 slice_bitcast_fusion.6
  79.9 0.0 all-reduce.5.cloned.1.call-update
  80.0 0.0 all-reduce.7.cloned.1.call-start
  80.0 95.0 %all-reduce.5.cloned.1.call-done = (f32[2,256,256]{2,1,0:T(8,128)}, f32[2,256,256]{2,1,0:T(8,128)}, f32[2,256,512]{2,1,0:T(8,128)}, f32[2,256,512]{2,1,0:T(8,128)}) async-done(((f32[2,256,256]{2,1,0:T(8,128)}, f32[2,256,256]{2,1,0:T(8,128)}, f32[2,256,512]{2,1,0:T(8,128)}, f32[2,256,512]{2,1,0:T(8,128)}), (f32[2,256,256]{2,1,0:T(8,128)}, f32[2,256,256]{2,1,0:T(8,128)}, f32[2,256,512]{2,1,0:T(8,128)}, ...) | async-done | bytes 3145744 | tf_op jit(solution)/shard_map/psum | solution.py:27
  175.0 0.0 all-reduce.7.cloned.1.call-update
  175.0 88.9 %all-reduce.7.cloned.1.call-done = (f32[2,256,256]{2,1,0:T(8,128)}, f32[2,256,256]{2,1,0:T(8,128)}, f32[2,256,512]{2,1,0:T(8,128)}, f32[2,256,512]{2,1,0:T(8,128)}) async-done(((f32[2,256,256]{2,1,0:T(8,128)}, f32[2,256,256]{2,1,0:T(8,128)}, f32[2,256,512]{2,1,0:T(8,128)}, f32[2,256,512]{2,1,0:T(8,128)}), (f32[2,256,256]{2,1,0:T(8,128)}, f32[2,256,256]{2,1,0:T(8,128)}, f32[2,256,512]{2,1,0:T(8,128)}, ...) | async-done | bytes 3145744 | tf_op jit(solution)/shard_map/psum | solution.py:27
  264.0 1.4 constant_dynamic-update-slice_fusion.4
  265.4 0.1 copy-done.5
  265.5 0.1 maximum_bitcast_fusion
  265.5 0.7 copy-done.1
  266.2 0.6 fusion.13
  266.8 0.6 fusion.12
  267.5 0.0 copy-start.2
  267.5 0.6 fusion.2
  268.1 0.6 fusion.3
  268.8 0.2 copy-done.3
  269.0 0.3 maximum_subtract_fusion
  269.3 0.0 copy-start
  269.4 1.1 fusion.11
  270.4 1.1 fusion.10
  271.5 1.1 convolution_add_fusion.1
  272.6 1.1 convolution_subtract_fusion.1
  273.6 1.0 fusion.15
  274.6 1.0 fusion.14
  275.7 1.0 fusion.1
  276.7 1.0 fusion
  277.8 0.2 pad_maximum_fusion
  278.0 2.4 reshape_reshape.3
  280.4 2.8 copy.17
  283.2 60.7 %all_to_all.20 = f32[64,8,2,512]{3,2,1,0:T(2,128)S(1)} all-to-all(f32[64,8,2,512]{3,2,1,0:T(2,128)S(1)} %bitcast.143), channel_id=1, replica_groups=mesh['row_0'=8,'row_1'=4,'col_0'=8,'col_1'=2] {'row_1','col_0','col_1'}, dimensions={0} | all-to-all | bytes 4194304 | tf_op jit(solution)/shard_map/all_to_all | solution.py:38
  343.9 0.7 reduce_sum.18
  344.6 13.2 %all_to_all.21 = f32[8,2,512]{2,1,0:T(2,128)S(1)} all-to-all(f32[8,2,512]{2,1,0:T(2,128)S(1)} %reduce_sum.18), channel_id=1, replica_groups=mesh['row_0'=8,'row_1'=4,'col_0'=8,'col_1'=2] {'row_0'}, dimensions={0} | all-to-all | bytes 65536 | tf_op jit(solution)/shard_map/all_to_all | solution.py:45
  357.8 9.2 %all_to_all.22 = f32[8,2,512]{2,1,0:T(2,128)S(1)} all-to-all(f32[8,2,512]{2,1,0:T(2,128)S(1)} %broadcast_in_dim.4), channel_id=1, replica_groups=mesh['row_0'=8,'row_1'=4,'col_0'=8,'col_1'=2] {'row_0'}, dimensions={0} | all-to-all | bytes 65536 | tf_op jit(solution)/shard_map/all_to_all | solution.py:55
  367.1 1.0 broadcast_in_dim.5
  368.1 59.3 %all_to_all.23 = f32[64,8,2,512]{3,2,1,0:T(2,128)S(1)} all-to-all(f32[64,8,2,512]{3,2,1,0:T(2,128)S(1)} %broadcast_in_dim.5), channel_id=1, replica_groups=mesh['row_0'=8,'row_1'=4,'col_0'=8,'col_1'=2] {'row_1','col_0','col_1'}, dimensions={0} | all-to-all | bytes 4194304 | tf_op jit(solution)/shard_map/all_to_all | solution.py:55
  427.4 0.8 copy.14
  428.2 2.4 reshape_reshape_reshape.3
  (15 shorter events, 0.1 us)
Async XLA Ops:
  7.2 17.7 %copy-start.6 = (f32[2,16,256]{2,1,0:T(8,128)S(1)}, f32[2,16,256]{2,1,0:T(8,128)}, u32[]{:S(2)}) copy-start(f32[2,16,256]{2,1,0:T(8,128)} %param.6) | copy-start | bytes 98308
  7.2 17.7 %copy-start.8 = (f32[2,16,512]{2,1,0:T(8,128)S(1)}, f32[2,16,512]{2,1,0:T(8,128)}, u32[]{:S(2)}) copy-start(f32[2,16,512]{2,1,0:T(8,128)} %param.9) | copy-start | bytes 196612
  7.2 67.7 %all-gather.2.cloned.1.call-start = ((), (), s32[]{:S(2)}) async-start(), calls=%async_computation.4 | async-start | bytes 2228224 | tf_op jit(solution)/shard_map/all_gather | solution.py:17
  24.9 0.7 copy-start.7
  25.6 149.4 %all-reduce.5.cloned.1.call-start = ((), (), s32[]{:S(2)}) async-start(), calls=%async_computation.5 | async-start | bytes 6291456 | tf_op jit(solution)/shard_map/psum | solution.py:27
  80.0 184.0 %all-reduce.7.cloned.1.call-start = ((), (), s32[]{:S(2)}) async-start(), calls=%async_computation.6 | async-start | bytes 6291456 | tf_op jit(solution)/shard_map/psum | solution.py:27
  264.0 1.5 copy-start.4
  264.0 1.5 copy-start.5
  264.0 2.2 copy-start.1
  267.5 1.3 copy-start.2
  267.5 1.5 copy-start.3
  269.3 3.2 copy-start
Sparse Core Ops, SparseCore 0:
  25.7 49.1 all-gather.1
  80.1 94.8 all-reduce.4
  177.6 86.3 all-reduce.6
where the time goes:
time: 438 us; the launch traced here: 437 us
  waiting for transfers between devices  233 us (53%)
  blocking collectives  142 us (32%)
  matrix products  27 us (6%)
  between operations  14 us (3%)
  local copies, waits for them, and re-layouts  13.2 us (3%)
  other arithmetic  7.14 us (2%)
    psum x2, waiting for transfers between devices, broadcast_by_axis(): x = lax.psum(x, axis)  184 us
    all_to_all x2, blocking collectives, copy_for_each(): lax.all_to_all(jnp.broadcast_to(x[None], (peers, *x.shape)), axis, 0, 0,...  68.6 us
    all_to_all x1, blocking collectives, summed_on_arrival(): lax.all_to_all(blocks, axis, split_axis=0, concat_axis=0, tiled=True)  60.7 us
    all_gather x1, waiting for transfers between devices, sent_together(): lax.all_gather(both, axis, axis=dim, tiled=True)  49.2 us
    dot_general x28, matrix products, real_dot(): jnp.dot(left, right, precision=HIGH, preferred_element_type=jnp.float32)  27 us
    all_to_all x1, blocking collectives, summed_rows(): return jnp.sum(lax.all_to_all(own, far, 0, 0, tiled=True), axis=0)  13.2 us
  transfers between devices with their start and end apart: 3, of which 3 were waited for; matrix products, arithmetic and copies ran while one was open for 0% of the time, Pallas kernels for 0%

commit v1 on v0

v1 whole, which is shorter than its diff:
```python
import functools

import jax
import jax.numpy as jnp
from jax import lax
from jax.experimental import pallas as pl
from jax.experimental.pallas import tpu as pltpu
from jax.sharding import PartitionSpec as P

MESH = pl.DeviceIdType.MESH
HIGH = lax.Precision.HIGHEST
F32 = jnp.float32
BF16 = jnp.bfloat16
NY, NX, NZ = 8, 4, 8
PA, PC = 2, 4
NP = PA + PC
L = 128
ORDERS = ("yxz", "xyz", "xyz", "xyz")


def split(v):
    hi = v.astype(BF16)
    return hi, (v - hi.astype(F32)).astype(BF16)


def bdot(a, b, nt=False):
    dims = (((1,), (1 if nt else 0,)), ((), ()))
    return lax.dot_general(a, b, dims, preferred_element_type=F32)


def dot3(a, b, nt=False):
    (ah, al), (bh, bl) = a, b
    return bdot(ah, bh, nt) + (bdot(ah, bl, nt) + bdot(al, bh, nt))


def hdot(a, b, nt=False):
    dims = (((1,), (1 if nt else 0,)), ((), ()))
    return lax.dot_general(a, b, dims, precision=HIGH, preferred_element_type=F32)


def chdot(a, b, nt=False):
    (ar, ai), (br, bi) = a, b
    return (
        hdot(ar, br, nt) - hdot(ai, bi, nt),
        hdot(ar, bi, nt) + hdot(ai, br, nt),
    )


def kernel(
    front_hbm, panel, inverses, coupling, channels, schur_hbm, proj_hbm,
    front, schur, own, ybuf, col, row, s_hi, s_lo, ct_hi, ct_lo, x_hi, x_lo,
    part, sib_in, acc1, in1, acc2, in2, acc3, in3, whole,
    y_s, y_r, z_s, z_r, x_s, x_r, c_s, c_r, w_s, w_r, wc_s, wc_r,
    ps_s, ps_r, r1_s, r1_r, r2_s, r2_r, e_s, e_r, g2_s, g2_r, g1_s, g1_r, f_s, f_r, local_sem,
):
    r = lax.axis_index("row")
    c = lax.axis_index("col")
    y, x, z, k = r // NX, lax.rem(r, NX), c // 2, lax.rem(c, 2)
    other = 1 - k

    def at(yy, xx, zz, kk):
        return (yy * NX + xx, zz * 2 + kk)

    def up(v, d, n):
        return lax.rem(v + (d + n), n)

    def peer(axis, d):
        if axis == "y":
            return at(up(y, d, NY), x, z, k)
        if axis == "x":
            return at(y, up(x, d, NX), z, k)
        return at(y, x, up(z, d, NZ), k)

    sibling = at(y, x, z, other)
    index = {"y": y, "x": x, "z": z}
    size = {"y": NY, "x": NX, "z": NZ}
    sent = []

    def send(src, dst, s, r_, dev):
        copy = pltpu.make_async_remote_copy(
            src_ref=src, dst_ref=dst, send_sem=s, recv_sem=r_, device_id=dev, device_id_type=MESH
        )
        copy.start()
        return copy

    def arrived(ref, sem):
        pltpu.make_async_copy(ref, ref, sem).wait()

    barrier = pltpu.get_barrier_semaphore()
    greeted = [sibling]
    greeted += [peer("y", d) for d in range(1, NY)]
    greeted += [peer("z", d) for d in range(1, NZ)]
    greeted += [peer("x", d) for d in range(1, NX)]
    for dev in greeted:
        pl.semaphore_signal(barrier, inc=1, device_id=dev, device_id_type=MESH)

    load_front = pltpu.make_async_copy(front_hbm, front, local_sem.at[0])
    load_front.start()
    for p in range(NP):
        if p < PA:
            own[p] = panel[:, :, p * L : (p + 1) * L]
        else:
            own[p] = channels[:, :, (p - PA) * L : (p - PA + 1) * L]
    pl.semaphore_wait(barrier, len(greeted))

    near_first = (1, 7, 2, 6, 3, 5, 4)
    on_diagonal = y == z

    def y_send(p):
        @pl.when(on_diagonal)
        def _():
            for d in near_first:
                send(own.at[p], col.at[p, x, :, z, k], y_s.at[p, d], y_r.at[p, d], peer("y", d))
            pltpu.make_async_copy(own.at[p], col.at[p, x, :, z, k], local_sem.at[1 + p]).start()

        @pl.when(jnp.logical_not(on_diagonal))
        def _():
            for d in near_first:
                send(own.at[p], ybuf.at[p, y], y_s.at[p, d], y_r.at[p, d], peer("y", d))
            send(own.at[p], col.at[p, x, :, z, k], z_s.at[p, y], z_r.at[p, z], at(y, x, y, k))

    def y_drain(p):
        for d in near_first:
            arrived(own.at[p], y_s.at[p, d])

    def z_step(p):
        for d in near_first:
            yy = up(y, -d, NY)
            arrived(own.at[p], y_r.at[p, d])

            @pl.when(yy != z)
            def _():
                send(ybuf.at[p, yy], col.at[p, x, :, z, k], z_s.at[p, yy], z_r.at[p, z], at(y, x, yy, k))

    def z_drain(p):
        for yy in range(NY):
            @pl.when(yy != z)
            def _():
                arrived(own.at[p], z_s.at[p, yy])

    right, left = up(x, 1, NX), up(x, -1, NX)

    def x_step(p):
        for d in (1, 7, 2, 6, 3, 5, 4):
            arrived(own.at[p], z_r.at[p, up(z, -d, NZ)])

        @pl.when(on_diagonal)
        def _():
            pltpu.make_async_copy(own.at[p], own.at[p], local_sem.at[1 + p]).wait()

        line = col.at[p, x, :, :, k]
        send(line, line, x_s.at[p, 0], x_r.at[p, 0], peer("x", 1))
        send(line, line, x_s.at[p, 1], x_r.at[p, 1], peer("x", -1))

    def half(p, xx, h):
        return col.at[p, xx, :, pl.ds(h * (NZ // 2), NZ // 2), k]

    def x_forward(p):
        arrived(col.at[p, left, :, :, k], x_r.at[p, 0])
        send(half(p, left, 0), half(p, left, 0), x_s.at[p, 2], x_r.at[p, 2], peer("x", 1))
        arrived(col.at[p, right, :, :, k], x_r.at[p, 1])
        send(half(p, right, 1), half(p, right, 1), x_s.at[p, 3], x_r.at[p, 3], peer("x", -1))

    def x_drain(p):
        for n in range(2):
            arrived(col.at[p, x, :, :, k], x_s.at[p, n])
            arrived(half(p, x, 0), x_s.at[p, 2 + n])

    def pair(p, kk):
        return col.at[p, pl.ds(2 * (1 - kk), 2), :, :, kk]

    def sib_step(p):
        arrived(half(p, x, 0), x_r.at[p, 2])
        arrived(half(p, x, 1), x_r.at[p, 3])
        send(pair(p, k), pair(p, k), c_s.at[p], c_r.at[p], sibling)

    def sib_wait(p):
        arrived(pair(p, other), c_r.at[p])

    def sib_drain(p):
        arrived(pair(p, k), c_s.at[p])

    spans = (pl.ds(0, PA), pl.ds(PA, PC))

    def row_part(g, zz, comp=None):
        if comp is None:
            return row.at[spans[g], :, zz, k]
        return row.at[spans[g], comp, zz, k]

    def row_own(g):
        pltpu.make_async_copy(own.at[spans[g]], row_part(g, z), local_sem.at[8 + g]).start()
        send(own.at[spans[g]], row_part(g, z), w_s.at[g, 0, 0], w_r.at[g, 0, 0], peer("z", 1))
        send(own.at[spans[g]], row_part(g, z), w_s.at[g, 0, 1], w_r.at[g, 0, 1], peer("z", -1))

    def row_ring(g, step):
        for way, sign in ((0, 1), (1, -1)):
            zz = up(z, -sign * step, NZ)
            arrived(row_part(g, zz), w_r.at[g, step - 1, way])
            comp = way if step == 3 else None
            part_ = row_part(g, zz, comp)
            send(part_, part_, w_s.at[g, step, way], w_r.at[g, step, way], peer("z", sign))

    def row_sib(g):
        for way in (0, 1):
            arrived(row_part(g, up(z, 4, NZ), way), w_r.at[g, 3, way])
        pltpu.make_async_copy(own.at[spans[g]], row_part(g, z), local_sem.at[8 + g]).wait()
        both = row.at[spans[g], :, :, k]
        send(both, both, wc_s.at[g], wc_r.at[g], sibling)

    def row_wait(g):
        arrived(row.at[spans[g], :, :, other], wc_r.at[g])

    def row_drain(g):
        for step in range(4):
            for way in (0, 1):
                comp = way if step == 3 else None
                arrived(row_part(g, z, comp), w_s.at[g, step, way])
        arrived(row.at[spans[g], :, :, k], wc_s.at[g])

    def make_g():
        inv0 = (inverses[0, 0], inverses[0, 1])
        inv1 = (inverses[1, 0], inverses[1, 1])
        m = chdot(inv0, (coupling[0], coupling[1]), nt=True)
        n = chdot(m, inv1)
        nm = chdot(n, m, nt=True)
        im = chdot(inv1, m, nt=True)

        def block(i):
            top = jnp.concatenate([inv0[i] + nm[i], -n[i]], axis=1)
            return jnp.concatenate([top, jnp.concatenate([-im[i], inv1[i]], axis=1)], axis=0)

        gr, gi = block(0), block(1)
        return jnp.concatenate(
            [jnp.concatenate([gr, gi], axis=1), jnp.concatenate([-gi, gr], axis=1)], axis=0
        )

    def row_cat():
        parts = [row[p, i].reshape(NZ * 2 * 16, L) for i in range(2) for p in range(PA)]
        return jnp.concatenate(parts, axis=1)

    def make_scaled(g):
        scaled = hdot(row_cat(), g)
        xr, xi = scaled[:, : PA * L], scaled[:, PA * L :]
        both = jnp.concatenate(
            [jnp.concatenate([xr, -xi], axis=1), jnp.concatenate([xi, xr], axis=1)], axis=0
        )
        x_hi[...], x_lo[...] = split(both)

    def make_schur():
        for l in range(2):
            xx = 2 * k + l
            parts = [col[p, xx, i].reshape(256, L) for i in range(2) for p in range(PA)]
            a = split(jnp.concatenate(parts, axis=1))
            update = dot3((x_hi[...], x_lo[...]), a, nt=True)
            for i in range(2):
                s = front[i, :, l * 256 : (l + 1) * 256] - update[i * 256 : (i + 1) * 256]
                schur[i, :, l * 256 : (l + 1) * 256] = s
                hi, lo = split(s)
                s_hi[i * 256 : (i + 1) * 256, l * 256 : (l + 1) * 256] = hi
                s_lo[i * 256 : (i + 1) * 256, l * 256 : (l + 1) * 256] = lo

    def make_ct():
        for i in range(2):
            for j in range(PC):
                t = row[PA + j, i].reshape(256, L).T
                hi, lo = split(t)
                ct_hi[i * 512 + j * L : i * 512 + (j + 1) * L] = hi
                ct_lo[i * 512 + j * L : i * 512 + (j + 1) * L] = lo

    def make_part(j):
        p = PA + j
        lines = []
        for l in range(2):
            xx = 2 * k + l
            lines.append(jnp.concatenate([col[p, xx, i].reshape(256, L) for i in range(2)], axis=1))
        b = split(jnp.concatenate(lines, axis=0))
        t = dot3((s_hi[...], s_lo[...]), b)
        ar = t[:256, :L] - t[256:, L:]
        ai = t[:256, L:] + t[256:, :L]
        q = dot3((ct_hi[...], ct_lo[...]), split(jnp.concatenate([ar, ai], axis=1)))
        part[j, 0] = q[:512, :L] - q[512:, L:]
        part[j, 1] = q[:512, L:] + q[512:, :L]

    def p_sib(j):
        send(part.at[j, other], sib_in.at[j], ps_s.at[j], ps_r.at[j], sibling)

    def dims(j):
        a, b, e = ORDERS[j]
        return a, b, e, 512 // size[a], 512 // size[a] // size[b]

    def rs1(j):
        a, b, e, h1, h2 = dims(j)
        arrived(sib_in.at[j], ps_r.at[j])
        acc1[j] = part[j, k] + sib_in[j]
        for d in range(1, size[a]):
            to = up(index[a], d, size[a])
            send(
                acc1.at[j, pl.ds(to * h1, h1)], in1.at[j, pl.ds(d * h1, h1)],
                r1_s.at[j, d], r1_r.at[j, d], peer(a, d),
            )

    def rs2(j):
        a, b, e, h1, h2 = dims(j)
        total = acc1[j, pl.ds(index[a] * h1, h1)]
        for d in range(1, size[a]):
            arrived(in1.at[j, pl.ds(d * h1, h1)], r1_r.at[j, d])
            total = total + in1[j, d * h1 : (d + 1) * h1]
        acc2[j, :h1] = total
        for d in range(1, size[b]):
            to = up(index[b], d, size[b])
            send(
                acc2.at[j, pl.ds(to * h2, h2)], in2.at[j, pl.ds(d * h2, h2)],
                r2_s.at[j, d], r2_r.at[j, d], peer(b, d),
            )

    def exchange(j):
        a, b, e, h1, h2 = dims(j)
        total = acc2[j, pl.ds(index[b] * h2, h2)]
        for d in range(1, size[b]):
            arrived(in2.at[j, pl.ds(d * h2, h2)], r2_r.at[j, d])
            total = total + in2[j, d * h2 : (d + 1) * h2]
        in3[j, index[e], :h2] = total
        mine = in3.at[j, index[e], pl.ds(0, h2)]
        for d in range(1, size[e]):
            send(mine, mine, e_s.at[j, d], e_r.at[j, d], peer(e, d))

    def ag2(j):
        a, b, e, h1, h2 = dims(j)
        for d in range(1, size[e]):
            arrived(in3.at[j, up(index[e], -d, size[e]), pl.ds(0, h2)], e_r.at[j, d])
        total = in3[j, 0, :h2]
        for i in range(1, size[e]):
            total = total + in3[j, i, :h2]
        start = index[a] * h1 + index[b] * h2
        whole[j, k, pl.ds(start, h2)] = total
        mine = whole.at[j, k, pl.ds(start, h2)]
        for d in range(1, size[b]):
            send(mine, mine, g2_s.at[j, d], g2_r.at[j, d], peer(b, d))

    def ag1(j):
        a, b, e, h1, h2 = dims(j)
        for d in range(1, size[b]):
            frm = up(index[b], -d, size[b])
            arrived(whole.at[j, k, pl.ds(index[a] * h1 + frm * h2, h2)], g2_r.at[j, d])
        mine = whole.at[j, k, pl.ds(index[a] * h1, h1)]
        for d in range(1, size[a]):
            send(mine, mine, g1_s.at[j, d], g1_r.at[j, d], peer(a, d))

    def out(j, kk):
        return pltpu.make_async_copy(
            whole.at[j, kk], proj_hbm.at[kk, :, pl.ds(j * L, L)], local_sem.at[11 + 2 * j + kk]
        )

    def fin(j):
        a, b, e, h1, h2 = dims(j)
        for d in range(1, size[a]):
            frm = up(index[a], -d, size[a])
            arrived(whole.at[j, k, pl.ds(frm * h1, h1)], g1_r.at[j, d])
        send(whole.at[j, k], whole.at[j, k], f_s.at[j], f_r.at[j], sibling)

    def fin_wait(j):
        arrived(whole.at[j, other], f_r.at[j])
        for kk in range(2):
            out(j, kk).start()

    def sum_drain(j):
        a, b, e, h1, h2 = dims(j)
        arrived(sib_in.at[j], ps_s.at[j])
        arrived(sib_in.at[j], f_s.at[j])
        for d in range(1, size[a]):
            arrived(in1.at[j, pl.ds(0, h1)], r1_s.at[j, d])
            arrived(in1.at[j, pl.ds(0, h1)], g1_s.at[j, d])
        for d in range(1, size[b]):
            arrived(in1.at[j, pl.ds(0, h2)], r2_s.at[j, d])
            arrived(in1.at[j, pl.ds(0, h2)], g2_s.at[j, d])
        for d in range(1, size[e]):
            arrived(in1.at[j, pl.ds(0, h2)], e_s.at[j, d])

    y_send(0)
    row_own(0)
    y_send(1)
    row_own(1)
    for p in range(2, NP):
        y_send(p)
    g = make_g()
    z_step(0)
    row_ring(0, 1)
    z_step(1)
    row_ring(0, 2)
    x_step(0)
    row_ring(0, 3)
    row_ring(1, 1)
    z_step(2)
    x_step(1)
    x_forward(0)
    row_sib(0)
    z_step(3)
    row_ring(1, 2)
    x_step(2)
    x_forward(1)
    sib_step(0)
    row_wait(0)
    make_scaled(g)
    z_step(4)
    row_ring(1, 3)
    x_step(3)
    x_forward(2)
    sib_step(1)
    z_step(5)
    x_step(4)
    row_sib(1)
    load_front.wait()
    sib_wait(0)
    sib_wait(1)
    make_schur()
    store_schur = pltpu.make_async_copy(schur, schur_hbm, local_sem.at[10])
    store_schur.start()
    row_wait(1)
    make_ct()
    x_forward(3)
    sib_step(2)
    x_step(5)
    x_forward(4)
    sib_step(3)
    sib_wait(2)
    make_part(0)
    p_sib(0)
    x_forward(5)
    sib_step(4)
    sib_wait(3)
    make_part(1)
    p_sib(1)
    rs1(0)
    sib_step(5)
    sib_wait(4)
    make_part(2)
    p_sib(2)
    rs2(0)
    rs1(1)
    sib_wait(5)
    make_part(3)
    p_sib(3)
    exchange(0)
    rs2(1)
    rs1(2)

    ag2(0)
    exchange(1)
    rs2(2)
    rs1(3)

    ag1(0)
    ag2(1)
    exchange(2)
    rs2(3)

    fin(0)
    ag1(1)
    ag2(2)
    exchange(3)

    fin_wait(0)
    fin(1)
    ag1(2)
    ag2(3)

    fin_wait(1)
    fin(2)
    ag1(3)

    fin_wait(2)
    fin(3)
    fin_wait(3)

    for p in range(NP):
        y_drain(p)
        z_drain(p)
        x_drain(p)
        sib_drain(p)
    for q in range(2):
        row_drain(q)
    for j in range(PC):
        sum_drain(j)
    store_schur.wait()
    for j in range(PC):
        for kk in range(2):
            out(j, kk).wait()


def local(front, panel, inverses, coupling, channels):
    any_, vmem = pl.BlockSpec(memory_space=pl.ANY), pl.BlockSpec(memory_space=pltpu.VMEM)
    dma = pltpu.SemaphoreType.DMA
    v = pltpu.VMEM
    scratch = [
        v((2, 256, 512), F32),
        v((2, 256, 512), F32),
        v((NP, 2, 16, L), F32),
        v((NP, NY, 2, 16, L), F32),
        v((NP, NX, 2, NZ, 2, 16, L), F32),
        v((NP, 2, NZ, 2, 16, L), F32),
        v((512, 512), BF16), v((512, 512), BF16),
        v((1024, 256), BF16), v((1024, 256), BF16),
        v((512, 512), BF16), v((512, 512), BF16),
        v((PC, 2, 512, L), F32),
        v((PC, 512, L), F32),
        v((PC, 512, L), F32), v((PC, 512, L), F32),
        v((PC, 128, L), F32), v((PC, 128, L), F32),
        v((PC, 8, L), F32), v((PC, 8, 16, L), F32),
        v((PC, 2, 512, L), F32),
        dma((NP, 8)), dma((NP, 8)), dma((NP, 8)), dma((NP, 8)),
        dma((NP, 4)), dma((NP, 4)), dma((NP,)), dma((NP,)),
        dma((2, 4, 2)), dma((2, 4, 2)), dma((2,)), dma((2,)),
        dma((PC,)), dma((PC,)),
        dma((PC, 8)), dma((PC, 8)), dma((PC, 8)), dma((PC, 8)),
        dma((PC, 8)), dma((PC, 8)), dma((PC, 8)), dma((PC, 8)),
        dma((PC, 8)), dma((PC, 8)), dma((PC,)), dma((PC,)),
        dma((20,)),
    ]
    return pl.pallas_call(
        kernel,
        out_shape=(
            jax.ShapeDtypeStruct((2, 256, 512), F32),
            jax.ShapeDtypeStruct((2, 512, 512), F32),
        ),
        in_specs=[any_, vmem, vmem, vmem, vmem],
        out_specs=(any_, any_),
        scratch_shapes=scratch,
        compiler_params=pltpu.CompilerParams(
            collective_id=0, has_side_effects=True, vmem_limit_bytes=48 * 2**20
        ),
        cost_estimate=pl.CostEstimate(flops=4 * 10**9, bytes_accessed=8 * 2**20, transcendentals=0),
    )(front, panel, inverses, coupling, channels)


def solution(mesh):
    in_specs = (P(None, "row", "col"), P(None, ("row", "col"), None), P(), P(), P(None, ("row", "col"), None))
    out_specs = (P(None, "row", "col"), P())
    return jax.shard_map(local, mesh=mesh, in_specs=in_specs, out_specs=out_specs, check_vma=False)
```

time: 438 us -> 124 us (0.28)
  waiting for transfers between devices: 233 us -> 0 us
  blocking collectives: 142 us -> 0 us
  Pallas kernels: 0 us -> 116 us
  matrix products: 27 us -> 0 us
  between operations: 14 us -> 0.65 us
  other arithmetic: 7.14 us -> 0 us
  local copies, waits for them, and re-layouts: 13.2 us -> 6.96 us
    psum x2 -> x0, waiting for transfers between devices: 184 us -> none  [broadcast_by_axis(): x = lax.psum(x, axis)]
    all_to_all x4 -> x0, blocking collectives: 142 us -> none  [the longest x2 68.6 us: copy_for_each(): lax.all_to_all(jnp.broadcast_to(x[None], (peers, *x.shape)), axis, 0, 0,...]
    pallas_call x0 -> x1, Pallas kernels: none -> 116 us  [local(): pl.pallas_call(kernel, out_shape=(jax.ShapeDtypeStruct((2, 256, 512), F32...]
    all_gather x1 -> x0, waiting for transfers between devices: 49.2 us -> none  [sent_together(): lax.all_gather(both, axis, axis=dim, tiled=True)]
    dot_general x28 -> x0, matrix products: 27 us -> none  [real_dot(): jnp.dot(left, right, precision=HIGH, preferred_element_type=jnp.float32)]
    another operation x3 -> x0, local copies, waits for them, and re-layouts: 7.66 us -> none  [the longest x2 5.22 us: in_blocks(): return jnp.moveaxis(x.reshape(*before, peers, -1, *after), dim, 0)]
  transfers between devices with their start and end apart: 3 -> 0, of which waited for: 3 -> 0; matrix products, arithmetic and copies ran while one was open for 0% -> 0% of each run, Pallas kernels for 0% -> 0%
where the time goes in v1:
time: 124 us
  Pallas kernels  116 us (94%)
  local copies, waits for them, and re-layouts  6.96 us (6%)
    pallas_call x1, Pallas kernels, local(): pl.pallas_call(kernel, out_shape=(jax.ShapeDtypeStruct((2, 256, 512), F32...  116 us
    unnamed x12, local copies, waits for them, and re-layouts  6.96 us

profile of v1, /device:TPU:1, one launch (start us, length us, event | category | flops | bytes accessed | tf_op | source)
XLA Modules:
  0.0 123.8 jit_solution(13697744851051945709)
XLA Ops:
  0.6 0.0 copy-start
  0.6 1.2 copy-done
  1.9 0.0 copy-start.1
  1.9 0.9 copy-done.1
  2.8 0.0 copy-start.2
  2.8 0.9 copy-done.2
  3.7 0.0 copy-start.3
  3.7 0.8 copy-done.3
  4.6 0.0 copy-start.4
  4.6 0.8 copy-done.4
  5.3 116.2 %shard_map.68 = (f32[2,256,512]{2,1,0:T(8,128)S(1)}, f32[2,512,512]{2,1,0:T(8,128)S(1)}) custom-call(f32[2,256,512]{2,1,0:T(8,128)S(1)} %copy-done, f32[2,16,256]{2,1,0:T(8,128)S(1)} %copy-done.4, f32[2,2,128,128]{3,2,1,0:T(8,128)S(1)} %copy-done.1, f32[2,128,128]{2,1,0:T(8,128)S(1)} %copy-done.2, f32[2,16,512]{2,1,0:T(8,128)S(1)} %copy-done.3), custom_call_target="tpu_custom_call" | custom-call | flops 4000000000 | bytes 8388608 | tf_op jit(solution)/shard_map/pallas_call | solution.py:519
  121.5 1.0 copy.9
  122.5 1.3 %copy.10 = f32[2,512,512]{2,1,0:T(8,128)} copy(f32[2,512,512]{2,1,0:T(8,128)S(1)} %get-tuple-element.5) | data formatting | bytes 4194304
Async XLA Ops:
  0.6 1.2 copy-start
  1.9 0.9 copy-start.1
  2.8 0.9 copy-start.2
  3.7 0.8 copy-start.3
  4.6 0.8 copy-start.4

commit v2 on v1

v2 whole, which is shorter than its diff:
```python
import functools

import jax
import jax.numpy as jnp
from jax import lax
from jax.experimental import pallas as pl
from jax.experimental.pallas import tpu as pltpu
from jax.sharding import PartitionSpec as P

MESH = pl.DeviceIdType.MESH
HIGH = lax.Precision.HIGHEST
F32 = jnp.float32
BF16 = jnp.bfloat16
NY, NX, NZ = 8, 4, 8
PA, PC = 2, 4
NP = PA + PC
L = 128
PLANES = ("y", "z")
MEMBERS = 32
SLICE = 256 // MEMBERS


def split(v):
    hi = v.astype(BF16)
    return hi, (v - hi.astype(F32)).astype(BF16)


def bdot(a, b, nt=False):
    dims = (((1,), (1 if nt else 0,)), ((), ()))
    return lax.dot_general(a, b, dims, preferred_element_type=F32)


def dot3(a, b, nt=False):
    (ah, al), (bh, bl) = a, b
    return bdot(ah, bh, nt) + (bdot(ah, bl, nt) + bdot(al, bh, nt))


def hdot(a, b, nt=False):
    dims = (((1,), (1 if nt else 0,)), ((), ()))
    return lax.dot_general(a, b, dims, precision=HIGH, preferred_element_type=F32)


def chdot(a, b, nt=False):
    (ar, ai), (br, bi) = a, b
    return (
        hdot(ar, br, nt) - hdot(ai, bi, nt),
        hdot(ar, bi, nt) + hdot(ai, br, nt),
    )


def kernel(
    front_hbm, panel_hbm, inverses_hbm, coupling_hbm, channels_hbm, schur_hbm, proj_hbm,
    front, schur, inverses, coupling, own, mine, col, row, s_hi, s_lo, ct_hi, ct_lo, x_hi, x_lo,
    part, sib_in, acc, scat, exch, whole,
    g_s, g_r, x_s, x_r, f_s, w_s, w_r, wc_s, wc_r,
    ps_s, ps_r, rs_s, rs_r, e_s, e_r, ag_s, ag_r, fin_s, fin_r, local_sem, out_sem,
):
    r = lax.axis_index("row")
    c = lax.axis_index("col")
    y, x, z, k = r // NX, lax.rem(r, NX), c // 2, lax.rem(c, 2)
    other = 1 - k

    def at(yy, xx, zz, kk):
        return (yy * NX + xx, zz * 2 + kk)

    def up(v, d, n):
        return lax.rem(v + (d + n), n)

    sibling = at(y, x, z, other)
    user = x // 2
    odd = lax.rem(x, 2)
    on_diagonal = y == z

    def send(src, dst, s, r_, dev):
        copy = pltpu.make_async_remote_copy(
            src_ref=src, dst_ref=dst, send_sem=s, recv_sem=r_, device_id=dev, device_id_type=MESH
        )
        copy.start()

    def bring(src, dst, sem):
        pltpu.make_async_copy(src, dst, sem).start()

    def arrived(ref, sem):
        pltpu.make_async_copy(ref, ref, sem).wait()

    for p in range(NP):
        src, q = (panel_hbm, p) if p < PA else (channels_hbm, p - PA)
        bring(src.at[:, :, pl.ds(q * L, L)], own.at[p], local_sem.at[p])
    bring(inverses_hbm, inverses, local_sem.at[6])
    bring(coupling_hbm, coupling, local_sem.at[7])
    bring(front_hbm, front, local_sem.at[8])

    barrier = pltpu.get_barrier_semaphore()

    def greet(dev):
        pl.semaphore_signal(barrier, inc=1, device_id=dev, device_id_type=MESH)

    greet(sibling)
    for zz in range(NZ):

        @pl.when(jnp.logical_not(jnp.logical_and(on_diagonal, zz == z)))
        def _():
            greet(at(z, x, zz, k))

    near = 2 * k + 1 - odd
    for kk in range(2):
        greet(at(y, near, z, kk))

    def plane_peer(axis, d, e):
        xx = up(x, e, NX)
        if axis == "y":
            return at(up(y, d, NY), xx, z, k)
        return at(y, xx, up(z, d, NZ), k)

    def for_plane(one):
        for e in range(1, NX):
            one(e, 0, e)

        def step(d, carry):
            for e in range(NX):
                one(d * NX + e, d, e)
            return carry

        lax.fori_loop(1, NY, step, 0)

    def greet_plane(axis):
        for_plane(lambda n, d, e: greet(plane_peer(axis, d, e)))

    greet_plane("y")
    greet_plane("z")
    n_yz = jnp.where(on_diagonal, NY - 1, NY)
    pl.semaphore_wait(barrier, 1 + n_yz + 2 + 2 * (MEMBERS - 1))

    for p in range(NP):
        arrived(own.at[p], local_sem.at[p])

    near_first = (0, 1, 7, 2, 6, 3, 5, 4)

    def g_send(p):
        dst = mine.at[p, :, z]
        for d in near_first[1:]:
            send(own.at[p], dst, g_s.at[p], g_r.at[p], at(up(y, d, NY), x, y, k))

        @pl.when(on_diagonal)
        def _():
            bring(own.at[p], dst, g_r.at[p])

        @pl.when(jnp.logical_not(on_diagonal))
        def _():
            send(own.at[p], dst, g_s.at[p], g_r.at[p], at(y, x, y, k))

    def g_drain(p):
        arrived(mine.at[p, :, pl.ds(0, NY - 1)], g_s.at[p])

        @pl.when(jnp.logical_not(on_diagonal))
        def _():
            arrived(own.at[p], g_s.at[p])

    def x_step(p):
        arrived(mine.at[p], g_r.at[p])
        dst, sem = col.at[p, odd, :, :, k], x_r.at[p, odd, k]
        send(mine.at[p], dst, x_s.at[p], sem, at(y, up(x, 1, NX), z, user))
        send(mine.at[p], dst, x_s.at[p], sem, at(y, up(x, -1, NX), z, user))

        @pl.when(user == k)
        def _():
            bring(mine.at[p], dst, sem)

        @pl.when(user != k)
        def _():
            send(mine.at[p], dst, x_s.at[p], sem, sibling)

    def x_drain(p):
        arrived(mine.at[p], x_s.at[p])
        arrived(mine.at[p], x_s.at[p])

        @pl.when(user != k)
        def _():
            arrived(mine.at[p], x_s.at[p])

    from_left = near == up(x, -1, NX)
    h = jnp.where(from_left, 0, 1)
    beyond = at(y, jnp.where(from_left, up(x, 1, NX), up(x, -1, NX)), z, k)

    def x_forward(p):
        for kk in range(2):
            arrived(mine.at[p], x_r.at[p, 1 - odd, kk])
        part_ = col.at[p, 1 - odd, :, pl.ds(h * (NZ // 2), NZ // 2)]
        send(part_, part_, f_s.at[p], x_r.at[p, 1 - odd, h], beyond)

    def x_wait(p):
        for kk in range(2):
            arrived(mine.at[p], x_r.at[p, odd, kk])

    def f_drain(p):
        arrived(mine.at[p], f_s.at[p])

    spans = (pl.ds(0, PA), pl.ds(PA, PC))

    def along_z(d):
        return at(y, x, up(z, d, NZ), k)

    def row_part(g, zz, comp=None):
        if comp is None:
            return row.at[spans[g], :, zz, k]
        return row.at[spans[g], comp, zz, k]

    def row_own(g):
        bring(own.at[spans[g]], row_part(g, z), local_sem.at[9 + g])
        send(own.at[spans[g]], row_part(g, z), w_s.at[g, 0, 0], w_r.at[g, 0, 0], along_z(1))
        send(own.at[spans[g]], row_part(g, z), w_s.at[g, 0, 1], w_r.at[g, 0, 1], along_z(-1))

    def row_ring(g, step):
        for way, sign in ((0, 1), (1, -1)):
            zz = up(z, -sign * step, NZ)
            arrived(row_part(g, zz), w_r.at[g, step - 1, way])
            part_ = row_part(g, zz, way if step == 3 else None)
            send(part_, part_, w_s.at[g, step, way], w_r.at[g, step, way], along_z(sign))

    def row_sib(g):
        for way in (0, 1):
            arrived(row_part(g, up(z, 4, NZ), way), w_r.at[g, 3, way])
        arrived(own.at[spans[g]], local_sem.at[9 + g])
        both = row.at[spans[g], :, :, k]
        send(both, both, wc_s.at[g], wc_r.at[g], sibling)

    def row_wait(g):
        arrived(row.at[spans[g], :, :, other], wc_r.at[g])

    def row_drain(g):
        for step in range(4):
            for way in (0, 1):
                comp = way if step == 3 else None
                arrived(row_part(g, z, comp), w_s.at[g, step, way])
        arrived(row.at[spans[g], :, :, k], wc_s.at[g])

    def make_g():
        arrived(inverses, local_sem.at[6])
        arrived(coupling, local_sem.at[7])
        inv0 = (inverses[0, 0], inverses[0, 1])
        inv1 = (inverses[1, 0], inverses[1, 1])
        m = chdot(inv0, (coupling[0], coupling[1]), nt=True)
        n = chdot(m, inv1)
        nm = chdot(n, m, nt=True)
        im = chdot(inv1, m, nt=True)

        def block(i):
            top = jnp.concatenate([inv0[i] + nm[i], -n[i]], axis=1)
            return jnp.concatenate([top, jnp.concatenate([-im[i], inv1[i]], axis=1)], axis=0)

        gr, gi = block(0), block(1)
        return jnp.concatenate(
            [jnp.concatenate([gr, gi], axis=1), jnp.concatenate([-gi, gr], axis=1)], axis=0
        )

    def row_cat():
        parts = [row[p, i].reshape(NZ * 2 * 16, L) for i in range(2) for p in range(PA)]
        return jnp.concatenate(parts, axis=1)

    def make_scaled(g):
        scaled = hdot(row_cat(), g)
        xr, xi = scaled[:, : PA * L], scaled[:, PA * L :]
        both = jnp.concatenate(
            [jnp.concatenate([xr, -xi], axis=1), jnp.concatenate([xi, xr], axis=1)], axis=0
        )
        x_hi[...], x_lo[...] = split(both)

    def make_schur():
        for l in range(2):
            parts = [col[p, l, i].reshape(256, L) for i in range(2) for p in range(PA)]
            a = split(jnp.concatenate(parts, axis=1))
            update = dot3((x_hi[...], x_lo[...]), a, nt=True)
            for i in range(2):
                s = front[i, :, l * 256 : (l + 1) * 256] - update[i * 256 : (i + 1) * 256]
                schur[i, :, l * 256 : (l + 1) * 256] = s
                hi, lo = split(s)
                s_hi[i * 256 : (i + 1) * 256, l * 256 : (l + 1) * 256] = hi
                s_lo[i * 256 : (i + 1) * 256, l * 256 : (l + 1) * 256] = lo

    def make_ct():
        for i in range(2):
            for j in range(PC):
                t = row[PA + j, i].reshape(256, L).T
                hi, lo = split(t)
                ct_hi[i * 512 + j * L : i * 512 + (j + 1) * L] = hi
                ct_lo[i * 512 + j * L : i * 512 + (j + 1) * L] = lo

    def make_part(j):
        p = PA + j
        lines = []
        for l in range(2):
            lines.append(jnp.concatenate([col[p, l, i].reshape(256, L) for i in range(2)], axis=1))
        b = split(jnp.concatenate(lines, axis=0))
        t = dot3((s_hi[...], s_lo[...]), b)
        ar = t[:256, :L] - t[256:, L:]
        ai = t[:256, L:] + t[256:, :L]
        q = dot3((ct_hi[...], ct_lo[...]), split(jnp.concatenate([ar, ai], axis=1)))
        part[j, 0] = q[:512, :L] - q[512:, L:]
        part[j, 1] = q[:512, L:] + q[512:, :L]

    position = {"y": y * NX + x, "z": z * NX + x}
    along = {"y": y, "z": z}

    def rows(h, i):
        return pl.ds(pl.multiple_of(h * 256 + i * SLICE, SLICE), SLICE)

    def p_sib(j):
        send(part.at[j, other], sib_in.at[j], ps_s.at[j], ps_r.at[j], sibling)

    def rs(j):
        arrived(sib_in.at[j], ps_r.at[j])
        acc[j] = part[j, k] + sib_in[j]

        def one(n, d, e):
            for h, axis in enumerate(PLANES):
                to = up(along[axis], d, NY) * NX + up(x, e, NX)
                send(
                    acc.at[j, rows(h, to)], scat.at[j, h, n], rs_s.at[j], rs_r.at[j, h],
                    plane_peer(axis, d, e),
                )

        for_plane(one)

    def exchange(j):
        for h, axis in enumerate(PLANES):
            arrived(scat.at[j, h, pl.ds(1, MEMBERS - 1)], rs_r.at[j, h])
            total = acc[j, rows(h, position[axis])]
            for n in range(1, MEMBERS):
                total = total + scat[j, h, n]
            i = z if axis == "y" else y
            exch[j, h, i] = total
            mine_ = exch.at[j, h, i]
            for d in (1, 7, 2, 6, 3, 5, 4):
                dev = at(y, x, up(z, d, NZ), k) if axis == "y" else at(up(y, d, NY), x, z, k)
                send(mine_, mine_, e_s.at[j], e_r.at[j, h], dev)

    def ag(j):
        for h, axis in enumerate(PLANES):
            arrived(exch.at[j, h, pl.ds(0, NZ - 1)], e_r.at[j, h])
            total = exch[j, h, 0]
            for i in range(1, NZ):
                total = total + exch[j, h, i]
            whole[j, k, rows(h, position[axis])] = total

        def one(n, d, e):
            for h, axis in enumerate(PLANES):
                mine_ = whole.at[j, k, rows(h, position[axis])]
                send(mine_, mine_, ag_s.at[j], ag_r.at[j], plane_peer(axis, d, e))

        for_plane(one)

    def out(j, kk):
        return pltpu.make_async_copy(
            whole.at[j, kk], proj_hbm.at[kk, :, pl.ds(j * L, L)], out_sem.at[j, kk]
        )

    def fin(j):
        arrived(scat.at[j, :, pl.ds(1, MEMBERS - 1)], ag_r.at[j])
        send(whole.at[j, k], whole.at[j, k], fin_s.at[j], fin_r.at[j], sibling)
        out(j, k).start()

    def fin_wait(j):
        arrived(whole.at[j, other], fin_r.at[j])
        out(j, other).start()

    def sum_drain(j):
        arrived(sib_in.at[j], ps_s.at[j])
        arrived(sib_in.at[j], fin_s.at[j])
        arrived(scat.at[j, :, pl.ds(1, MEMBERS - 1)], rs_s.at[j])
        arrived(scat.at[j, :, pl.ds(1, MEMBERS - 1)], ag_s.at[j])
        arrived(exch.at[j, :, pl.ds(0, NZ - 1)], e_s.at[j])

    g_send(0)
    g_send(1)
    row_own(0)
    g = make_g()
    x_step(0)
    g_send(2)
    row_ring(0, 1)
    x_step(1)
    g_send(3)
    row_ring(0, 2)
    row_own(1)
    x_step(2)
    x_forward(0)
    g_send(4)
    row_ring(0, 3)
    x_step(3)
    x_forward(1)
    g_send(5)
    row_ring(1, 1)
    row_sib(0)
    x_step(4)
    x_forward(2)
    row_ring(1, 2)
    row_wait(0)
    make_scaled(g)
    x_step(5)
    x_forward(3)
    row_ring(1, 3)
    x_wait(0)
    x_wait(1)
    arrived(front, local_sem.at[8])
    make_schur()
    bring(schur, schur_hbm, local_sem.at[11])
    row_sib(1)
    x_forward(4)
    x_wait(2)
    row_wait(1)
    make_ct()
    make_part(0)
    p_sib(0)
    x_wait(3)
    make_part(1)
    p_sib(1)
    rs(0)
    x_forward(5)
    x_wait(4)
    make_part(2)
    p_sib(2)
    rs(1)
    exchange(0)
    rs(2)
    x_wait(5)
    make_part(3)
    p_sib(3)
    exchange(1)
    ag(0)
    rs(3)
    exchange(2)
    ag(1)
    exchange(3)
    ag(2)
    fin(0)
    ag(3)
    fin(1)
    fin_wait(0)
    fin(2)
    fin_wait(1)
    fin(3)
    fin_wait(2)
    fin_wait(3)

    for p in range(NP):
        g_drain(p)
        x_drain(p)
        f_drain(p)
    for q in range(2):
        row_drain(q)
    for j in range(PC):
        sum_drain(j)
    arrived(schur, local_sem.at[11])
    for j in range(PC):
        for kk in range(2):
            out(j, kk).wait()


def local(front, panel, inverses, coupling, channels):
    hbm = pl.BlockSpec(memory_space=pltpu.HBM)
    dma = pltpu.SemaphoreType.DMA
    v = pltpu.VMEM
    scratch = [
        v((2, 256, 512), F32),
        v((2, 256, 512), F32),
        v((2, 2, 128, 128), F32),
        v((2, 128, 128), F32),
        v((NP, 2, 16, L), F32),
        v((NP, 2, NZ, 16, L), F32),
        v((NP, 2, 2, NZ, 2, 16, L), F32),
        v((NP, 2, NZ, 2, 16, L), F32),
        v((512, 512), BF16), v((512, 512), BF16),
        v((1024, 256), BF16), v((1024, 256), BF16),
        v((512, 512), BF16), v((512, 512), BF16),
        v((PC, 2, 512, L), F32),
        v((PC, 512, L), F32), v((PC, 512, L), F32),
        v((PC, 2, MEMBERS, SLICE, L), F32),
        v((PC, 2, NZ, SLICE, L), F32),
        v((PC, 2, 512, L), F32),
        dma((NP,)), dma((NP,)),
        dma((NP,)), dma((NP, 2, 2)), dma((NP,)),
        dma((2, 4, 2)), dma((2, 4, 2)), dma((2,)), dma((2,)),
        dma((PC,)), dma((PC,)), dma((PC,)), dma((PC, 2)), dma((PC,)), dma((PC, 2)),
        dma((PC,)), dma((PC,)), dma((PC,)), dma((PC,)),
        dma((12,)), dma((PC, 2)),
    ]
    return pl.pallas_call(
        kernel,
        out_shape=(
            jax.ShapeDtypeStruct((2, 256, 512), F32),
            jax.ShapeDtypeStruct((2, 512, 512), F32),
        ),
        in_specs=[hbm] * 5,
        out_specs=(hbm, hbm),
        scratch_shapes=scratch,
        compiler_params=pltpu.CompilerParams(
            collective_id=0, has_side_effects=True, vmem_limit_bytes=56 * 2**20
        ),
        cost_estimate=pl.CostEstimate(flops=4 * 10**9, bytes_accessed=8 * 2**20, transcendentals=0),
    )(front, panel, inverses, coupling, channels)


def solution(mesh):
    in_specs = (P(None, "row", "col"), P(None, ("row", "col"), None), P(), P(), P(None, ("row", "col"), None))
    out_specs = (P(None, "row", "col"), P())
    return jax.shard_map(local, mesh=mesh, in_specs=in_specs, out_specs=out_specs, check_vma=False)
```

time: 124 us -> 101 us (0.81)
  Pallas kernels: 116 us -> 96.9 us
  local copies, waits for them, and re-layouts: 6.96 us -> 3.73 us
    pallas_call x1, Pallas kernels: 116 us -> 96.9 us  [local(): pl.pallas_call(kernel, out_shape=(jax.ShapeDtypeStruct((2, 256, 512), F32...]
    unnamed x12 -> x4, local copies, waits for them, and re-layouts: 6.96 us -> 3.73 us
where the time goes in v2:
time: 101 us
  Pallas kernels  96.9 us (96%)
  local copies, waits for them, and re-layouts  3.73 us (4%)
    pallas_call x1, Pallas kernels, local(): pl.pallas_call(kernel, out_shape=(jax.ShapeDtypeStruct((2, 256, 512), F32...  96.9 us
    unnamed x4, local copies, waits for them, and re-layouts  3.73 us

profile of v2, /device:TPU:1, one launch (start us, length us, event | category | flops | bytes accessed | tf_op | source)
XLA Modules:
  0.0 101.3 jit_solution(3810685561047686562)
XLA Ops:
  0.6 96.9 %shard_map.68 = (f32[2,256,512]{2,1,0:T(8,128)}, f32[2,512,512]{2,1,0:T(8,128)}) custom-call(f32[2,256,512]{2,1,0:T(8,128)} %front_hbm.1, f32[2,16,256]{2,1,0:T(8,128)} %panel_hbm.1, f32[2,2,128,128]{3,2,1,0:T(8,128)} %inverses_hbm.1, f32[2,128,128]{2,1,0:T(8,128)} %coupling_hbm.1, f32[2,16,512]{2,1,0:T(8,128)} %channels_hbm.1), custom_call_target="tpu_custom_call" | custom-call | flops 4000000000 | bytes 8388608 | tf_op jit(solution)/shard_map/pallas_call | solution.py:486
  97.5 0.0 copy-start
  97.5 2.4 %copy.9 = f32[2,256,512]{2,1,0:T(8,128)} copy(f32[2,256,512]{2,1,0:T(8,128)} %get-tuple-element.4) | data formatting | bytes 2097152
  99.9 0.0 copy-done
  99.9 1.3 %copy.10 = f32[2,512,512]{2,1,0:T(8,128)} copy(f32[2,512,512]{2,1,0:T(8,128)S(1)} %copy-done) | data formatting | bytes 4194304
Async XLA Ops:
  97.5 2.4 %copy-start = (f32[2,512,512]{2,1,0:T(8,128)S(1)}, f32[2,512,512]{2,1,0:T(8,128)}, u32[]{:S(2)}) copy-start(f32[2,512,512]{2,1,0:T(8,128)} %get-tuple-element.5) | copy-start | bytes 6291460

commit v3 on v2

--- a/solution.py
+++ b/solution.py
@@ -349,19 +349,19 @@
 
         for_plane(one)
 
-    def out(j, kk):
-        return pltpu.make_async_copy(
-            whole.at[j, kk], proj_hbm.at[kk, :, pl.ds(j * L, L)], out_sem.at[j, kk]
-        )
+    def out_place(j):
+        return proj_hbm.at[k, :, pl.ds(j * L, L)]
+
+    def out(j):
+        return pltpu.make_async_copy(whole.at[j, k], out_place(j), out_sem.at[j])
 
     def fin(j):
         arrived(scat.at[j, :, pl.ds(1, MEMBERS - 1)], ag_r.at[j])
-        send(whole.at[j, k], whole.at[j, k], fin_s.at[j], fin_r.at[j], sibling)
-        out(j, k).start()
+        send(whole.at[j, k], out_place(j), fin_s.at[j], fin_r.at[j], sibling)
+        out(j).start()
 
     def fin_wait(j):
-        arrived(whole.at[j, other], fin_r.at[j])
-        out(j, other).start()
+        arrived(sib_in.at[j], fin_r.at[j])
 
     def sum_drain(j):
         arrived(sib_in.at[j], ps_s.at[j])
@@ -425,19 +425,19 @@
     make_part(3)
     p_sib(3)
     exchange(1)
+    rs(3)
     ag(0)
-    rs(3)
     exchange(2)
     ag(1)
     exchange(3)
     ag(2)
+    ag(3)
     fin(0)
-    ag(3)
     fin(1)
+    fin(2)
+    fin(3)
     fin_wait(0)
-    fin(2)
     fin_wait(1)
-    fin(3)
     fin_wait(2)
     fin_wait(3)
 
@@ -451,8 +451,7 @@
         sum_drain(j)
     arrived(schur, local_sem.at[11])
     for j in range(PC):
-        for kk in range(2):
-            out(j, kk).wait()
+        out(j).wait()
 
 
 def local(front, panel, inverses, coupling, channels):
@@ -481,7 +480,7 @@
         dma((2, 4, 2)), dma((2, 4, 2)), dma((2,)), dma((2,)),
         dma((PC,)), dma((PC,)), dma((PC,)), dma((PC, 2)), dma((PC,)), dma((PC, 2)),
         dma((PC,)), dma((PC,)), dma((PC,)), dma((PC,)),
-        dma((12,)), dma((PC, 2)),
+        dma((12,)), dma((PC,)),
     ]
     return pl.pallas_call(
         kernel,

time: 101 us -> 97.8 us (0.968)
  Pallas kernels: 96.9 us -> 93.3 us
    pallas_call x1, Pallas kernels: 96.9 us -> 93.3 us  [local(): pl.pallas_call(kernel, out_shape=(jax.ShapeDtypeStruct((2, 256, 512), F32...]
where the time goes in v3:
time: 97.8 us; the launch traced here: 97.6 us
  Pallas kernels  93.3 us (95%)
  local copies, waits for them, and re-layouts  3.73 us (4%)
    pallas_call x1, Pallas kernels, local(): pl.pallas_call(kernel, out_shape=(jax.ShapeDtypeStruct((2, 256, 512), F32...  93.3 us
    unnamed x4, local copies, waits for them, and re-layouts  3.73 us

profile of v3, /device:TPU:1, one launch (start us, length us, event | category | flops | bytes accessed | tf_op | source)
XLA Modules:
  0.0 97.6 jit_solution(18232846296669475613)
XLA Ops:
  0.6 93.3 %shard_map.68 = (f32[2,256,512]{2,1,0:T(8,128)}, f32[2,512,512]{2,1,0:T(8,128)}) custom-call(f32[2,256,512]{2,1,0:T(8,128)} %front_hbm.1, f32[2,16,256]{2,1,0:T(8,128)} %panel_hbm.1, f32[2,2,128,128]{3,2,1,0:T(8,128)} %inverses_hbm.1, f32[2,128,128]{2,1,0:T(8,128)} %coupling_hbm.1, f32[2,16,512]{2,1,0:T(8,128)} %channels_hbm.1), custom_call_target="tpu_custom_call" | custom-call | flops 4000000000 | bytes 8388608 | tf_op jit(solution)/shard_map/pallas_call | solution.py:485
  93.9 0.0 copy-start
  93.9 2.4 %copy.9 = f32[2,256,512]{2,1,0:T(8,128)} copy(f32[2,256,512]{2,1,0:T(8,128)} %get-tuple-element.4) | data formatting | bytes 2097152
  96.3 0.0 copy-done
  96.3 1.3 %copy.10 = f32[2,512,512]{2,1,0:T(8,128)} copy(f32[2,512,512]{2,1,0:T(8,128)S(1)} %copy-done) | data formatting | bytes 4194304
Async XLA Ops:
  93.9 2.4 %copy-start = (f32[2,512,512]{2,1,0:T(8,128)S(1)}, f32[2,512,512]{2,1,0:T(8,128)}, u32[]{:S(2)}) copy-start(f32[2,512,512]{2,1,0:T(8,128)} %get-tuple-element.5) | copy-start | bytes 6291460
